TPU v7x, 32 devices: a whole 2x2x4 slice. The times are simulated.
32 devices in a mesh: dp: 4 (over x, core), chan: 8 (over z, y).
Axes of the slice: x: 2, y: 2, z: 4, core: 2. Of those that a mesh axis runs over, the one named last changes fastest.
Arguments:
- tokens: bfloat16 [4096, 512], P('dp', 'chan'), may hold values from -6 to 6
- cotangent: float32 [4096, 512], P('dp', 'chan'), may hold values from -6 to 6
- group_bucket: int32 [4], P('dp'), may hold values from 0 to 2, as said below
- group_items: int32 [4], P('dp'), may hold values from 1 to 4, as said below
- first_norm_gain: float32 [512], P('chan'), may hold values from 0.5 to 1.5
- first_norm_bias: float32 [512], P('chan'), may hold values from -1 to 1
- modes: float32 [8, 512, 32], P(None, 'chan'), may hold values from -3 to 3
- log_dt: float32 [512], P('chan'), may hold values from -6.9 to -2.3
- d_skip: float32 [512], P('chan'), may hold values from -4 to 4
- w_a: float32 [512, 512], P('dp', 'chan'), may hold values from -0.25 to 0.25
- b_a: float32 [512], P('chan'), may hold values from -1 to 1
- w_b: float32 [512, 512], P('dp', 'chan'), may hold values from -0.25 to 0.25
- b_b: float32 [512], P('chan'), may hold values from -1 to 1
- second_norm_gain: float32 [512], P('chan'), may hold values from 0.5 to 1.5
- second_norm_bias: float32 [512], P('chan'), may hold values from -1 to 1
- w_up: float32 [512, 2048], P('dp', 'chan'), may hold values from -0.25 to 0.25
- b_up: float32 [2048], P('chan'), may hold values from -1 to 1
- w_down: float32 [2048, 512], P('chan', 'dp'), may hold values from -0.125 to 0.125
- b_down: float32 [512], P('chan'), may hold values from -1 to 1
Outputs:
- output: bfloat16 [4096, 512], P('dp', 'chan')
- grad_tokens: float32 [4096, 512], P('dp', 'chan')
- first_norm_gain_gradient: float32 [512], P('chan')
- grad_ln1_bias: float32 [512], P('chan')
- grad_modes: float32 [8, 512, 32], P(None, 'chan')
- grad_log_dt: float32 [512], P('chan')
- grad_d_skip: float32 [512], P('chan')
- grad_w_a: float32 [512, 512], P('dp', 'chan')
- grad_b_a: float32 [512], P('chan')
- grad_w_b: float32 [512, 512], P('dp', 'chan')
- grad_b_b: float32 [512], P('chan')
- second_norm_gain_gradient: float32 [512], P('chan')
- grad_ln2_bias: float32 [512], P('chan')
- grad_w_up: float32 [512, 2048], P('dp', 'chan')
- grad_b_up: float32 [2048], P('chan')
- grad_w_down: float32 [2048, 512], P('chan', 'dp')
- grad_b_down: float32 [512], P('chan')
Inputs may be any that keep to these rules, and one draw needn't show every extreme that they name: Data group g holds items of 256 * 2^group_bucket[g] tokens; some group is at level 2 and some at level 0 in every draw. `group_items`: A group at level b holds at least half of 4 // 2^b items and at most 4 // 2^b; some group holds one item of 1024 tokens and some other group four items in every draw.
All inputs are finite; a program needn't handle non-finite values.
Results may differ from a plain program's by a relative error of at most 0.0078.
Values may be sent and summed in bfloat16 or wider, within the bound.
A program may use at most 128 MiB of HBM per device.

v0:
```python
import math

import jax
import jax.numpy as jnp
import ml_dtypes
import numpy as np
from jax import lax
from jax.experimental import pallas as pl
from jax.experimental.pallas import tpu as pltpu
from jax.sharding import PartitionSpec as P

MODEL_WIDTH = 512
TOK_DEV = 1024


HIGHEST = lax.Precision.HIGHEST
EPSILON = 1e-05


def product(left, right):
    return jnp.dot(left, right, preferred_element_type=jnp.float32)


def product_nt(left, right):
    return lax.dot_general(
        left, right, (((1,), (1,)), ((), ())), preferred_element_type=jnp.float32
    )


def product_tn(left, right):
    return lax.dot_general(
        left, right, (((0,), (0,)), ((), ())), preferred_element_type=jnp.float32
    )


def gelu_slope(values):
    return (
        0.5 * (1.0 + lax.erf(values * 0.7071067811865476))
        + values * jnp.exp(-0.5 * values * values) * 0.3989422804014327
    )


def half_angles(length):
    angle = np.arange(length // 2 + 1, dtype=np.float64) * (math.pi / length)
    cosine, sine = np.cos(angle), np.sin(angle)
    cosine[-1] = 0.0
    return cosine.astype(np.float32), sine.astype(np.float32)


def inverse_tables(length):
    freq = np.arange(length // 2 + 1)
    turn = (freq[:, None] * np.arange(length)[None, :]) % length * (2.0 * math.pi / length)
    weight = np.where((freq == 0) | (freq == length // 2), 1.0, 2.0)[:, None] / length
    return (weight * np.cos(turn)).astype(np.float32), (weight * np.sin(turn)).astype(np.float32)


def high_einsum(form, left, right):
    return jnp.einsum(form, left, right, precision=HIGHEST)


def ssm_kernel(modes, log_dt):
    cos_h, sin_h = half_angles(TOK_DEV)
    index = jnp.arange(modes.shape[2], dtype=jnp.int32).astype(jnp.float32)
    lam_re = -0.5 * jnp.exp(modes[0])
    lam_im = math.pi * (index + modes[1])
    rank_re, rank_im, in_re, in_im, out_re, out_im = (modes[i] for i in range(2, 8))
    sigma = (2.0 * jnp.exp(-log_dt))[:, None]

    def points(values):
        return values.T[:, None, :]

    den_re = points(lam_re * lam_re + lam_im * lam_im) * (cos_h * cos_h)[:, None] - (
        sigma * sigma
    ).T * (sin_h * sin_h)[:, None]
    den_im = points(-2.0 * sigma * lam_re) * (sin_h * cos_h)[:, None]
    den_sq = den_re * den_re + den_im * den_im
    inv_re = den_re / den_sq
    inv_im = -den_im / den_sq
    sums = []
    for real, imag in (
        (out_re * in_re + out_im * in_im, out_re * in_im - out_im * in_re),
        (out_re * rank_re + out_im * rank_im, out_re * rank_im - out_im * rank_re),
        (rank_re * in_re + rank_im * in_im, rank_re * in_im - rank_im * in_re),
        (rank_re * rank_re + rank_im * rank_im, jnp.zeros_like(rank_re)),
    ):
        turned = points(real * lam_re + imag * lam_im)
        real = points(real)
        p_re, p_im = jnp.sum(real * inv_re, axis=0), jnp.sum(real * inv_im, axis=0)
        q_re, q_im = jnp.sum(turned * inv_re, axis=0), jnp.sum(turned * inv_im, axis=0)
        sine = sin_h[:, None] * sigma.T
        sums.append((-sine * p_im - cos_h[:, None] * q_re, sine * p_re - cos_h[:, None] * q_im))
    (cross_re, cross_im), (left_re, left_im), (right_re, right_im), (self_re, self_im) = sums
    twice = 2.0 * cos_h[:, None]
    loop_re, loop_im = 1.0 + twice * self_re, twice * self_im
    back_re, back_im = twice * right_re, twice * right_im
    loop_sq = loop_re * loop_re + loop_im * loop_im
    ratio_re = (back_re * loop_re + back_im * loop_im) / loop_sq
    ratio_im = (back_im * loop_re - back_re * loop_im) / loop_sq
    part_re = cross_re - (left_re * ratio_re - left_im * ratio_im)
    part_im = cross_im - (left_re * ratio_im + left_im * ratio_re)
    spec_re = 2.0 * (cos_h[:, None] * part_re - sin_h[:, None] * part_im)
    spec_im = 2.0 * (cos_h[:, None] * part_im + sin_h[:, None] * part_re)
    cos_tab, sin_tab = inverse_tables(TOK_DEV)
    return high_einsum("kl,kc->lc", cos_tab, spec_re) - high_einsum("kl,kc->lc", sin_tab, spec_im)


BLOCK = 128
BLOCKS = TOK_DEV // BLOCK
FIRST = 2 * BLOCKS
KEPT = FIRST // 2 + 1


def transform_tables():
    length = 2 * TOK_DEV
    turn = np.arange(KEPT)[:, None] * np.arange(BLOCK)[None, :] * (2.0 * math.pi / length)
    small = np.arange(BLOCK)[:, None] * np.arange(BLOCK)[None, :] % BLOCK * (2.0 * math.pi / BLOCK)
    spots = np.stack([np.arange(BLOCKS) + np.arange(BLOCKS) // (2 << b) * (2 << b) for b in range(3)])
    angle = spots[:, None, :] * np.arange(KEPT)[None, :, None] % FIRST * (2.0 * math.pi / FIRST)
    parts = (np.cos(turn), np.sin(turn), np.cos(small), np.sin(small), np.cos(angle), np.sin(angle))
    return [part.astype(np.float32) for part in parts]


def forward_transform(blocks, cos_a, sin_a):
    cos_t, sin_t, cos_s, sin_s, _, _ = transform_tables()
    step_re = high_einsum("ka,abc->kbc", cos_a, blocks)
    step_im = -high_einsum("ka,abc->kbc", sin_a, blocks)
    turned_re = step_re * cos_t[..., None] + step_im * sin_t[..., None]
    turned_im = step_im * cos_t[..., None] - step_re * sin_t[..., None]
    both = jnp.concatenate([turned_re, turned_im], axis=1)
    matrix = np.block([[cos_s, sin_s], [-sin_s, cos_s]])
    return high_einsum("pb,kbc->kpc", matrix, both)


def inverse_transform(spectrum, cos_a, sin_a):
    cos_t, sin_t, cos_s, sin_s, _, _ = transform_tables()
    matrix = np.block([[cos_s, -sin_s], [sin_s, cos_s]])
    both = high_einsum("bp,kpc->kbc", matrix, spectrum)
    step_re, step_im = both[:, :BLOCK], both[:, BLOCK:]
    turned_re = step_re * cos_t[..., None] - step_im * sin_t[..., None]
    turned_im = step_im * cos_t[..., None] + step_re * sin_t[..., None]
    weight = np.where(np.arange(KEPT) % (KEPT - 1) == 0, 1.0, 2.0).astype(np.float32) / (2 * TOK_DEV)
    return high_einsum("ka,kbc->abc", cos_a * weight[:, None], turned_re) - high_einsum(
        "ka,kbc->abc", sin_a * weight[:, None], turned_im
    )


def multiply(left, right):
    left_re, left_im = left[:, :BLOCK], left[:, BLOCK:]
    right_re, right_im = right[:, :BLOCK], right[:, BLOCK:]
    return jnp.concatenate(
        [left_re * right_re - left_im * right_im, left_re * right_im + left_im * right_re], axis=1
    )


def mixer(normed, kernel_taps, skip_gain, bucket, filled):
    _, _, _, _, cos_a, sin_a = transform_tables()
    cos_x, sin_x = jnp.asarray(cos_a)[bucket], jnp.asarray(sin_a)[bucket]
    item_blocks = 2 << bucket
    block_id = jnp.arange(BLOCKS, dtype=jnp.int32)[:, None, None]
    taps = jnp.where(block_id < item_blocks, kernel_taps.reshape(BLOCKS, BLOCK, -1), 0.0)
    signal = forward_transform(normed.reshape(BLOCKS, BLOCK, -1), cos_x, sin_x)
    answer = forward_transform(taps, cos_a[2], sin_a[2])
    result = inverse_transform(multiply(signal, answer), cos_x, sin_x)
    result = jnp.where(block_id < filled * item_blocks, result, 0.0)
    return result.reshape(normed.shape) + skip_gain * normed


def shards(
    tokens,
    cotangent,
    group_bucket,
    group_items,
    first_norm_gain,
    first_norm_bias,
    modes,
    log_dt,
    d_skip,
    w_a,
    b_a,
    w_b,
    b_b,
    second_norm_gain,
    second_norm_bias,
    w_up,
    b_up,
    w_down,
    b_down,
):
    input_tokens = tokens.astype(jnp.float32)
    sums_in = lax.psum(
        (jnp.sum(input_tokens, axis=1), jnp.sum(input_tokens * input_tokens, axis=1)), "chan"
    )
    input_average = sums_in[0][:, None] / MODEL_WIDTH
    input_inverse_deviation = lax.rsqrt(
        sums_in[1][:, None] / MODEL_WIDTH - input_average * input_average + EPSILON
    )
    input_standardized = (input_tokens - input_average) * input_inverse_deviation
    input_normalized = input_standardized * first_norm_gain + first_norm_bias
    level = group_bucket[0]
    filled = group_items[0]
    kernel_taps, kernel_back = jax.vjp(ssm_kernel, modes, log_dt)

    def local_mix(values, taps_now, skip_gain):
        return mixer(values, taps_now, skip_gain, level, filled)

    mixed, mix_back = jax.vjp(local_mix, input_normalized, kernel_taps, d_skip)
    acts_low = jax.nn.gelu(mixed, approximate=False).astype(jnp.bfloat16)
    wa_full, wb_full, up_full, down_full = (
        lax.all_gather(w_a.astype(jnp.bfloat16), "dp", axis=0, tiled=True),
        lax.all_gather(w_b.astype(jnp.bfloat16), "dp", axis=0, tiled=True),
        lax.all_gather(w_up.astype(jnp.bfloat16), "dp", axis=0, tiled=True),
        lax.all_gather(w_down.astype(jnp.bfloat16), "dp", axis=1, tiled=True),
    )
    acts_full = lax.all_gather(acts_low, "chan", axis=1, tiled=True)
    gate_a = product(acts_full, wa_full) + b_a
    gate_b = product(acts_full, wb_full) + b_b
    gate_sig = jax.nn.sigmoid(gate_b)
    residual_stream = input_tokens + gate_a * gate_sig
    sums_mid = lax.psum(
        (jnp.sum(residual_stream, axis=1), jnp.sum(residual_stream * residual_stream, axis=1)),
        "chan",
    )
    middle_average = sums_mid[0][:, None] / MODEL_WIDTH
    middle_inverse_deviation = lax.rsqrt(
        sums_mid[1][:, None] / MODEL_WIDTH - middle_average * middle_average + EPSILON
    )
    middle_standardized = (residual_stream - middle_average) * middle_inverse_deviation
    middle_reduced = (middle_standardized * second_norm_gain + second_norm_bias).astype(
        jnp.bfloat16
    )
    mid_full = lax.all_gather(middle_reduced, "chan", axis=1, tiled=True)
    pre_act = product(mid_full, up_full) + b_up
    hidden_low = jax.nn.gelu(pre_act, approximate=False).astype(jnp.bfloat16)
    branch = (
        lax.psum_scatter(product(hidden_low, down_full), "chan", scatter_dimension=1, tiled=True)
        + b_down
    )
    output = (residual_stream + branch).astype(jnp.bfloat16)
    grad_f = cotangent.astype(jnp.bfloat16)
    grad_b_down = jnp.sum(grad_f.astype(jnp.float32), axis=0)
    grad_f_full = lax.all_gather(grad_f, "chan", axis=1, tiled=True)
    grad_w_down = product_tn(hidden_low, grad_f_full)
    grad_pre = (product_nt(grad_f_full, down_full) * gelu_slope(pre_act)).astype(jnp.bfloat16)
    grad_b_up = jnp.sum(grad_pre.astype(jnp.float32), axis=0)
    grad_w_up = product_tn(mid_full, grad_pre)
    middle_gradient = lax.psum_scatter(
        product_nt(grad_pre, up_full), "chan", scatter_dimension=1, tiled=True
    )
    second_norm_gain_gradient = jnp.sum(middle_gradient * middle_standardized, axis=0)
    grad_ln2_bias = jnp.sum(middle_gradient, axis=0)
    middle_rescaled = middle_gradient * second_norm_gain
    middle_backward = lax.psum(
        (jnp.sum(middle_rescaled, axis=1), jnp.sum(middle_rescaled * middle_standardized, axis=1)),
        "chan",
    )
    grad_resid = cotangent + middle_inverse_deviation * (
        middle_rescaled
        - middle_backward[0][:, None] / MODEL_WIDTH
        - middle_standardized * middle_backward[1][:, None] / MODEL_WIDTH
    )
    grad_a = (grad_resid * gate_sig).astype(jnp.bfloat16)
    grad_b = (grad_resid * gate_a * gate_sig * (1.0 - gate_sig)).astype(jnp.bfloat16)
    grad_b_a = jnp.sum(grad_a.astype(jnp.float32), axis=0)
    grad_b_b = jnp.sum(grad_b.astype(jnp.float32), axis=0)
    grad_w_a = product_tn(acts_full, grad_a)
    grad_w_b = product_tn(acts_full, grad_b)
    grad_acts = lax.psum_scatter(
        product_nt(grad_a, wa_full) + product_nt(grad_b, wb_full),
        "chan",
        scatter_dimension=1,
        tiled=True,
    )
    grad_mixed = grad_acts * gelu_slope(mixed)
    normalized_gradient, grad_kernel, grad_skip = mix_back(grad_mixed)
    grad_modes, grad_log_dt = kernel_back(grad_kernel)
    first_norm_gain_gradient = jnp.sum(normalized_gradient * input_standardized, axis=0)
    grad_ln1_bias = jnp.sum(normalized_gradient, axis=0)
    input_rescaled = normalized_gradient * first_norm_gain
    input_backward = lax.psum(
        (jnp.sum(input_rescaled, axis=1), jnp.sum(input_rescaled * input_standardized, axis=1)),
        "chan",
    )
    grad_tokens = grad_resid + input_inverse_deviation * (
        input_rescaled
        - input_backward[0][:, None] / MODEL_WIDTH
        - input_standardized * input_backward[1][:, None] / MODEL_WIDTH
    )
    grad_w_a, grad_w_b, grad_w_up, grad_w_down = (
        lax.psum_scatter(grad_w_a, "dp", scatter_dimension=0, tiled=True),
        lax.psum_scatter(grad_w_b, "dp", scatter_dimension=0, tiled=True),
        lax.psum_scatter(grad_w_up, "dp", scatter_dimension=0, tiled=True),
        lax.psum_scatter(grad_w_down, "dp", scatter_dimension=1, tiled=True),
    )
    (
        first_norm_gain_gradient,
        grad_ln1_bias,
        grad_modes,
        grad_log_dt,
        grad_skip,
        grad_b_a,
        grad_b_b,
        second_norm_gain_gradient,
        grad_ln2_bias,
        grad_b_up,
        grad_b_down,
    ) = lax.psum(
        (
            first_norm_gain_gradient,
            grad_ln1_bias,
            grad_modes,
            grad_log_dt,
            grad_skip,
            grad_b_a,
            grad_b_b,
            second_norm_gain_gradient,
            grad_ln2_bias,
            grad_b_up,
            grad_b_down,
        ),
        "dp",
    )
    return (
        output,
        grad_tokens,
        first_norm_gain_gradient,
        grad_ln1_bias,
        grad_modes,
        grad_log_dt,
        grad_skip,
        grad_w_a,
        grad_b_a,
        grad_w_b,
        grad_b_b,
        second_norm_gain_gradient,
        grad_ln2_bias,
        grad_w_up,
        grad_b_up,
        grad_w_down,
        grad_b_down,
    )


LANES = 128
HALF = 64
PAIRS = 4
ROWS = 128
N_CHAN = 8
WIDE = 640
MESH = pl.DeviceIdType.MESH
F32 = jnp.float32
BF16 = jnp.bfloat16


def split_two(matrix):
    high = matrix.astype(ml_dtypes.bfloat16)
    low = (matrix - high.astype(np.float64)).astype(ml_dtypes.bfloat16)
    return np.concatenate([high, low], axis=1)


def lane_rows(values_low, values_high):
    return np.repeat(np.stack([values_low, values_high], -1), HALF, axis=-1)


def mixer_tables():
    line = np.arange(ROWS)
    small = np.outer(line, line) % ROWS * (2.0 * math.pi / ROWS)
    cos_s, sin_s = np.cos(small), np.sin(small)
    forward = np.block([[cos_s, sin_s], [-sin_s, cos_s]])
    real = np.zeros((2 * ROWS, 2 * ROWS))
    for row in range(HALF):
        weight = 1.0 if row == 0 else 2.0
        turn = 2.0 * math.pi / ROWS * row * line
        real[:ROWS, row] = weight * np.cos(turn)
        real[:ROWS, ROWS + row] = -weight * np.sin(turn)
        turn = 2.0 * math.pi / TOK_DEV * (4 + 8 * row) * line
        real[ROWS:, HALF + row] = 2.0 * np.cos(turn)
        real[ROWS:, ROWS + HALF + row] = -2.0 * np.sin(turn)
    mats = np.stack([split_two(m) for m in (forward, forward.T, real, real.T)])

    twiddle = []
    for pair in range(5):
        turn = np.stack([line * k * (math.pi / TOK_DEV) for k in (2 * pair, 2 * pair + 1)])
        twiddle += [lane_rows(np.cos(turn[0]), np.cos(turn[1])), lane_rows(np.sin(turn[0]), np.sin(turn[1]))]
    for first, second in ((1, 2), (3, 0)):
        turn = np.stack([line * k * (2.0 * math.pi / TOK_DEV) for k in (first, second)])
        twiddle += [lane_rows(np.cos(turn[0]), np.cos(turn[1])), lane_rows(np.sin(turn[0]), np.sin(turn[1]))]

    def forward_rows(coef, pairs):
        out = []
        for low, high in pairs:
            for part in range(2):
                for j in range(PAIRS):
                    out.append(lane_rows(coef(2 * j, low, part), coef(2 * j + 1, high, part)))
                for j in range(PAIRS):
                    out.append(lane_rows(coef(2 * j, high, part), coef(2 * j + 1, low, part)))
        return np.stack(out)

    def inverse_rows(coef, pairs):
        out = []
        for low, high in pairs:
            for part in range(2):
                for j in range(PAIRS):
                    out.append(lane_rows(coef(2 * j, low, part), coef(2 * j + 1, high, part)))
                for j in range(PAIRS):
                    out.append(lane_rows(coef(2 * j + 1, low, part), coef(2 * j, high, part)))
        return np.stack(out)

    levels = []
    pairs = [(2 * p, 2 * p + 1) for p in range(5)]
    for level in range(3):
        item = 2 << level

        def angle(block, k):
            return 2.0 * math.pi / 16 * ((block + block // item * item) * k % 16)

        def fwd(block, k, part):
            if k > 8:
                return np.zeros(())
            return np.cos(angle(block, k)) if part == 0 else -np.sin(angle(block, k))

        def inv(block, k, part):
            weight = (1.0 if k in (0, 8) else 2.0) / (2 * TOK_DEV)
            return weight * fwd(block, k, part)

        levels.append(np.concatenate([forward_rows(fwd, pairs), inverse_rows(inv, pairs)]))

    def taps(block, k, part):
        if k == 0:
            return np.asarray((1.0 if part == 0 else (-1.0) ** block) / TOK_DEV)
        turn = 2.0 * math.pi / 8 * (block * k % 8)
        return np.asarray((np.cos(turn) if part == 0 else -np.sin(turn)) * 2.0 / TOK_DEV)

    tap_pairs = [(1, 2), (3, 0)]
    taps_back = forward_rows(taps, tap_pairs)
    taps_rows = inverse_rows(taps, tap_pairs)
    freq_even = np.where(line < HALF, 8 * line, 4 + 8 * (line - HALF))
    half_angle = np.stack(
        [lane_rows(1 + 8 * line, 2 + 8 * line), lane_rows(3 + 8 * line, freq_even)]
    ) * (math.pi / TOK_DEV)
    wave = np.stack([np.cos(half_angle), np.sin(half_angle)])
    return (
        mats,
        np.stack(twiddle).astype(np.float32),
        np.stack(levels).astype(np.float32),
        np.concatenate([levels[2], taps_rows, taps_back]).astype(np.float32),
        wave.astype(np.float32),
    )


def low_lanes(rows):
    return lax.broadcasted_iota(jnp.int32, (rows, LANES), 1) < HALF


def turn_half(values):
    return pltpu.roll(values, HALF, 1)


def split_pair(values):
    upper, lower = values[:HALF], values[HALF:]
    mask = low_lanes(HALF)
    return jnp.where(mask, upper, turn_half(lower)), jnp.where(mask, turn_half(upper), lower)


def join_pair(first, second):
    mask = low_lanes(HALF)
    return jnp.concatenate(
        [jnp.where(mask, first, turn_half(second)), jnp.where(mask, turn_half(first), second)], axis=0
    )


def interleave(first, second):
    mask = low_lanes(first.shape[0])
    return jnp.where(mask, first, turn_half(second)), jnp.where(mask, turn_half(first), second)


def fold(values):
    return values + turn_half(values)


def reciprocal(values):
    guess = pl.reciprocal(values, approx=True)
    return guess * (2.0 - values * guess)


ERF_TERMS = (1.061405429, -1.453152027, 1.421413741, -0.284496736, 0.254829592)


def normal_parts(values):
    bell = jnp.exp(-0.5 * values * values)
    t = reciprocal(1.0 + (0.3275911 * 0.7071067811865476) * jnp.abs(values))
    tail = ERF_TERMS[0]
    for term in ERF_TERMS[1:]:
        tail = tail * t + term
    tail = 0.5 * (tail * t) * bell
    return jnp.where(values < 0.0, tail, 1.0 - tail), bell * 0.3989422804014327


def column_sum(values):
    return jnp.sum(values, axis=0, keepdims=True)


def dot_nt(left, right):
    return lax.dot_general(left, right, (((1,), (1,)), ((), ())), preferred_element_type=F32)


def dot_nn(left, right):
    return jnp.dot(left, right, preferred_element_type=F32)


def store_split(ref, row, lane, values, exact=True):
    high = values.astype(BF16)
    place = (pl.ds(row, values.shape[0]), pl.ds(lane, values.shape[1]))
    ref[(0,) + place] = high
    if exact:
        ref[(1,) + place] = (values - high.astype(F32)).astype(BF16)


def split_product(mat_ref, which, rhs_ref, lane, width, exact=True):
    high = mat_ref[which, :, 0:256]
    low = mat_ref[which, :, 256:512]
    rhs_high = rhs_ref[0, :, lane : lane + width]
    product = dot_nn(high, rhs_high) + dot_nn(low, rhs_high)
    if exact:
        product = product + dot_nn(high, rhs_ref[1, :, lane : lane + width])
    return product


CHUNK = 32


def over_chunks(body, size=CHUNK, first=0, rows=ROWS):
    def step(index, carry):
        body(pl.multiple_of(first + index * size, size))
        return carry

    lax.fori_loop(0, rows // size, step, 0)


def spread_pairs(src, coef_ref, base, twiddle_ref, twiddle_base, pairs, rhs_ref, exact=True):
    def body(row):
        rows = pl.ds(row, CHUNK)
        blocks = [src(j, rows) for j in range(PAIRS)]
        for pair in range(pairs):
            parts = []
            for part in range(2):
                at = base + (pair * 2 + part) * 8
                straight = sum(blocks[j] * coef_ref[at + j : at + j + 1, :] for j in range(PAIRS))
                crossed = sum(blocks[j] * coef_ref[at + 4 + j : at + 5 + j, :] for j in range(PAIRS))
                parts.append(straight + turn_half(crossed))
            cosine = twiddle_ref[twiddle_base + 2 * pair, rows, :]
            sine = twiddle_ref[twiddle_base + 2 * pair + 1, rows, :]
            store_split(rhs_ref, row, pair * LANES, parts[0] * cosine + parts[1] * sine, exact)
            store_split(rhs_ref, row + ROWS, pair * LANES, parts[1] * cosine - parts[0] * sine, exact)

    over_chunks(body)


def gather_pairs(values_ref, coef_ref, base, twiddle_ref, twiddle_base, pairs, store):
    def body(row):
        rows = pl.ds(row, CHUNK)
        straight, crossed = [0.0] * PAIRS, [0.0] * PAIRS
        for pair in range(pairs):
            lanes = slice(pair * LANES, (pair + 1) * LANES)
            real, imag = values_ref[rows, lanes], values_ref[pl.ds(row + ROWS, CHUNK), lanes]
            cosine = twiddle_ref[twiddle_base + 2 * pair, rows, :]
            sine = twiddle_ref[twiddle_base + 2 * pair + 1, rows, :]
            for part, value in enumerate((real * cosine - imag * sine, imag * cosine + real * sine)):
                at = base + (pair * 2 + part) * 8
                for j in range(PAIRS):
                    straight[j] = straight[j] + value * coef_ref[at + j : at + j + 1, :]
                    crossed[j] = crossed[j] + value * coef_ref[at + 4 + j : at + 5 + j, :]
        for j in range(PAIRS):
            store(j, rows, straight[j] + turn_half(crossed[j]))

    over_chunks(body)


GROUPS = ((0, 256), (256, 256), (512, 128))


def transform_into(dst_ref, mat_ref, which, rhs_ref, exact=True):
    for lane, width in GROUPS:
        dst_ref[:, lane : lane + width] = split_product(mat_ref, which, rhs_ref, lane, width, exact)


def multiply_spectra(left_ref, right_ref, rhs_ref, conjugate, exact=True):
    def body(row):
        top, bottom = pl.ds(row, CHUNK), pl.ds(row + ROWS, CHUNK)
        for pair in range(5):
            lanes = slice(pair * LANES, (pair + 1) * LANES)
            a_re, a_im = left_ref[top, lanes], left_ref[bottom, lanes]
            b_re, b_im = right_ref[top, lanes], right_ref[bottom, lanes]
            if conjugate:
                out_re, out_im = a_re * b_re + a_im * b_im, a_re * b_im - a_im * b_re
            else:
                out_re, out_im = a_re * b_re - a_im * b_im, a_re * b_im + a_im * b_re
            store_split(rhs_ref, row, pair * LANES, out_re, exact)
            store_split(rhs_ref, row + ROWS, pair * LANES, out_im, exact)

    over_chunks(body)


def pair_terms(modes_ref):
    rank_re, rank_im, in_re, in_im, out_re, out_im = (modes_ref[i] for i in range(2, 8))
    return (
        (out_re * in_re + out_im * in_im, out_re * in_im - out_im * in_re),
        (out_re * rank_re + out_im * rank_im, out_re * rank_im - out_im * rank_re),
        (rank_re * in_re + rank_im * in_im, rank_re * in_im - rank_im * in_re),
        (rank_re * rank_re + rank_im * rank_im, None),
    )


def mode_values(modes_ref):
    index = lax.broadcasted_iota(jnp.int32, modes_ref.shape[1:], 0).astype(F32)
    return -0.5 * jnp.exp(modes_ref[0]), math.pi * (index + modes_ref[1])


POINT_ROWS = 16


def resolvent(coef_ref, n, square_cos, cos_sin, scaled):
    den_re = coef_ref[8, pl.ds(n, 1), :] * square_cos - scaled
    den_im = coef_ref[9, pl.ds(n, 1), :] * cos_sin
    inverse = reciprocal(den_re * den_re + den_im * den_im)
    return den_re * inverse, -(den_im * inverse)


def complex_multiply(a_re, a_im, b_re, b_im):
    return a_re * b_re - a_im * b_im, a_re * b_im + a_im * b_re


def conj_multiply(a_re, a_im, b_re, b_im):
    return a_re * b_re + a_im * b_im, a_re * b_im - a_im * b_re


def combine(sums, sigma, cosine, sine):
    terms = []
    for p_re, p_im, q_re, q_im in (sums[4 * q : 4 * q + 4] for q in range(4)):
        swing = sigma * sine
        terms.append((-swing * p_im - cosine * q_re, swing * p_re - cosine * q_im))
    twice = 2.0 * cosine
    loop_re, loop_im = 1.0 + twice * terms[3][0], twice * terms[3][1]
    scale = reciprocal(loop_re * loop_re + loop_im * loop_im)
    inv = (loop_re * scale, -(loop_im * scale))
    ratio = complex_multiply(twice * terms[2][0], twice * terms[2][1], *inv)
    return terms, inv, ratio


QUARTER = 32


def cauchy_coefficients(modes_ref, sigma, coef_ref):
    lam_re, lam_im = mode_values(modes_ref)
    for q, (real, imag) in enumerate(pair_terms(modes_ref)):
        coef_ref[q] = real
        coef_ref[4 + q] = real * lam_re if imag is None else real * lam_re + imag * lam_im
    coef_ref[8] = lam_re * lam_re + lam_im * lam_im
    coef_ref[9] = -2.0 * sigma * lam_re


def wave_rows(wave_ref, pair, base, row):
    rows = pl.ds(pl.multiple_of(base + row, POINT_ROWS), POINT_ROWS)
    return wave_ref[0, pair, rows, :], wave_ref[1, pair, rows, :]


def cauchy_forward(index, sigma, coef_ref, wave_ref, base, sums_ref, spec_ref):
    sigma_sq = sigma * sigma
    pair, row = index // 2, index % 2 * POINT_ROWS
    rows = slice(row, row + POINT_ROWS)
    lanes = slice(pair * LANES, (pair + 1) * LANES)
    cosine, sine = wave_rows(wave_ref, pair, base, row)
    square_cos, cos_sin, scaled = cosine * cosine, cosine * sine, sigma_sq * (sine * sine)

    def add_mode(n, sums):
        sums = list(sums)
        for k in range(4):
            at = n * 4 + k
            inv_re, inv_im = resolvent(coef_ref, at, square_cos, cos_sin, scaled)
            for q in range(4):
                plain = coef_ref[q, pl.ds(at, 1), :]
                turned = coef_ref[4 + q, pl.ds(at, 1), :]
                sums[4 * q] = sums[4 * q] + plain * inv_re
                sums[4 * q + 1] = sums[4 * q + 1] + plain * inv_im
                sums[4 * q + 2] = sums[4 * q + 2] + turned * inv_re
                sums[4 * q + 3] = sums[4 * q + 3] + turned * inv_im
        return tuple(sums)

    zero = jnp.zeros((POINT_ROWS, LANES), F32)
    sums = lax.fori_loop(0, 8, add_mode, (zero,) * 16)
    for i in range(16):
        sums_ref[pair, i, rows, :] = sums[i]
    terms, _, ratio = combine(sums, sigma, cosine, sine)
    cut_re, cut_im = complex_multiply(*terms[1], *ratio)
    part_re, part_im = terms[0][0] - cut_re, terms[0][1] - cut_im
    spec_re, spec_im = complex_multiply(2.0 * cosine, 2.0 * sine, part_re, part_im)
    spec_ref[rows, lanes] = spec_re
    spec_ref[row + QUARTER : row + QUARTER + POINT_ROWS, lanes] = spec_im


PLACES = [(pair, row) for pair in range(2) for row in range(0, QUARTER, POINT_ROWS)]


def point_grads(sigma, wave_ref, base, sums_ref, spec_ref, grad_ref):
    zero = jnp.zeros((POINT_ROWS, LANES), F32)
    sigma_sum = zero
    for pair, row in PLACES:
        rows = slice(row, row + POINT_ROWS)
        lanes = slice(pair * LANES, (pair + 1) * LANES)
        cosine, sine = wave_rows(wave_ref, pair, base, row)
        sums = [sums_ref[pair, i, rows, :] for i in range(16)]
        terms, inv, ratio = combine(sums, sigma, cosine, sine)
        spec_re, spec_im = spec_ref[rows, lanes], spec_ref[row + QUARTER : row + QUARTER + POINT_ROWS, lanes]
        part = conj_multiply(2.0 * cosine, 2.0 * sine, spec_re, spec_im)
        left = conj_multiply(*ratio, *part)
        ratio_grad = conj_multiply(*terms[1], *part)
        back = conj_multiply(*inv, -ratio_grad[0], -ratio_grad[1])
        twice = 2.0 * cosine
        loop = conj_multiply(*ratio, *back)
        grads = (
            part,
            (-left[0], -left[1]),
            (twice * back[0], twice * back[1]),
            (-twice * loop[0], -twice * loop[1]),
        )
        swing = sigma * sine
        for q, (g_re, g_im) in enumerate(grads):
            grad_ref[pair, 4 * q, rows, :] = swing * g_im
            grad_ref[pair, 4 * q + 1, rows, :] = -swing * g_re
            grad_ref[pair, 4 * q + 2, rows, :] = -cosine * g_re
            grad_ref[pair, 4 * q + 3, rows, :] = -cosine * g_im
            sigma_sum = sigma_sum + sine * (g_im * sums[4 * q] - g_re * sums[4 * q + 1])
    return sigma_sum


def mode_sums(part, square_sum, sigma, coef_ref, wave_ref, base, grad_ref, back_ref):
    sigma_sq = sigma * sigma

    def mode(n, square_sum):
        plain = [coef_ref[q, pl.ds(n, 1), :] for q in range(4)]
        turned = [coef_ref[4 + q, pl.ds(n, 1), :] for q in range(4)]
        sums = [0.0] * 10
        for pair, row in PLACES:
            rows = slice(row, row + POINT_ROWS)
            cosine, sine = wave_rows(wave_ref, pair, base, row)
            square_cos, cos_sin, square_sin = cosine * cosine, cosine * sine, sine * sine
            inv_re, inv_im = resolvent(coef_ref, n, square_cos, cos_sin, sigma_sq * square_sin)
            grad_re, grad_im = 0.0, 0.0
            for q in range(4):
                p_re, p_im = grad_ref[pair, 4 * q, rows, :], grad_ref[pair, 4 * q + 1, rows, :]
                q_re, q_im = grad_ref[pair, 4 * q + 2, rows, :], grad_ref[pair, 4 * q + 3, rows, :]
                grad_re = grad_re + (plain[q] * p_re + turned[q] * q_re)
                grad_im = grad_im + (plain[q] * p_im + turned[q] * q_im)
                sums[q] = sums[q] + (p_re * inv_re + p_im * inv_im)
                sums[4 + q] = sums[4 + q] + (q_re * inv_re + q_im * inv_im)
            square_re = inv_re * inv_re - inv_im * inv_im
            square_im = 2.0 * inv_re * inv_im
            den_re, den_im = conj_multiply(square_re, square_im, grad_re, grad_im)
            sums[8] = sums[8] - den_re * square_cos
            sums[9] = sums[9] - den_im * cos_sin
            square_sum = square_sum + den_re * square_sin
        for i in range(10):
            back_ref[i, pl.ds(n, 1), :] = column_sum(sums[i])
        return square_sum

    return lax.fori_loop(part * 8, part * 8 + 8, mode, square_sum)


def mode_gradients(modes_ref, sigma, nyquist_grad, step, sigma_sum, square_sum, back_ref):
    plain_grad = [fold(back_ref[q]) for q in range(4)]
    turned_grad = [fold(back_ref[4 + q]) for q in range(4)]
    abs_grad, skew_grad = fold(back_ref[8]), fold(back_ref[9])
    lam_re, lam_im = mode_values(modes_ref)
    plain_grad[0] = plain_grad[0] + step * nyquist_grad
    rank_re, rank_im, in_re, in_im, out_re, out_im = (modes_ref[i] for i in range(2, 8))
    lam_re_grad = 2.0 * lam_re * abs_grad - 2.0 * sigma * skew_grad
    lam_im_grad = 2.0 * lam_im * abs_grad
    real_grad, imag_grad = [], []
    terms = pair_terms(modes_ref)
    for q, (real, imag) in enumerate(terms):
        lam_re_grad = lam_re_grad + turned_grad[q] * real
        if imag is not None:
            lam_im_grad = lam_im_grad + turned_grad[q] * imag
        real_grad.append(plain_grad[q] + turned_grad[q] * lam_re)
        imag_grad.append(turned_grad[q] * lam_im)
    r0, r1, r2, r3 = real_grad
    i0, i1, i2, _ = imag_grad
    grads = (
        lam_re_grad * lam_re,
        math.pi * lam_im_grad,
        r1 * out_re - i1 * out_im + r2 * in_re + i2 * in_im + 2.0 * r3 * rank_re,
        r1 * out_im + i1 * out_re + r2 * in_im - i2 * in_re + 2.0 * r3 * rank_im,
        r0 * out_re - i0 * out_im + r2 * rank_re - i2 * rank_im,
        r0 * out_im + i0 * out_re + r2 * rank_im + i2 * rank_re,
        r0 * in_re + i0 * in_im + r1 * rank_re + i1 * rank_im,
        r0 * in_im - i0 * in_re + r1 * rank_im - i1 * rank_re,
    )
    sigma_grad = (
        fold(column_sum(sigma_sum) + 2.0 * sigma * column_sum(square_sum))
        - 2.0 * column_sum(skew_grad * lam_re)
    )
    nyquist = step * column_sum(terms[0][0])
    return grads, nyquist * nyquist_grad - sigma * sigma_grad


def ring_place(chan):
    z, y = lax.div(chan, 2), lax.rem(chan, 2)
    return z + y * (7 - 2 * z)


def ring_chan(place):
    back = lax.div(place, 4)
    z = place * (1 - back) + (7 - place) * back
    return 2 * z + back


TURNS = (1, -1)


def block_kernel(
    loaded, bucket_ref, items_ref, tokens_ref, cotangent_ref, gain1_ref, bias1_ref, raw_modes_ref, log_dt_ref, skip_ref,
    wa_ref, ba_ref, wb_ref, bb_ref, gain2_ref, bias2_ref, up_ref, bup_ref, down_ref, bdown_ref,
    levels_ref, coefc_ref, mat_ref, tw_ref, wave_ref,
    out_ref, dtok_ref, gw_ref, gm_ref, gv_ref,
    tok_ref, aux_ref, coefl_ref, modes_ref,
    wab_ref, wh_ref, gab_w_ref, gh_ref,
    stage_ref, sib_ab_ref, ring_ab_ref, ring_h_ref, part_ab_ref, cross_ref, keep_ref, swap_ref, gate_total_ref,
    in_send, in_recv, head_send, head_recv, acts_send, acts_recv, back_send, back_recv, late_send, late_recv,
    sum_send, sum_recv, tail_send, dp_send, dp_low, dp_recv, spec_send, spec_recv, sgrad_send, sgrad_recv,
    hat_ref, norm_ref, slope_ref, conv_ref, rhs_ref, freq_ref, sig_ref, ans_ref, taps_ref,
    mcoef_ref, sums_ref, pgrad_ref, mback_ref, sgrad_ref, taps_freq_ref,
    gate_ref, swish_ref, res_ref, hat2_ref, acts_ref, norm2_ref, gradf_ref, branch_ref, back2_ref, half_send, half_recv,
    gab_ref, hid_ref, gpre_ref, acts_t_ref, norm2_t_ref, gradf_t_ref,
    gring_ss, gring_rs, gsib_ss, gsib_rs, gx_ss, gx_rs, gdx_ss, gdx_rs, gswap_ss, gswap_rs, core_ss, core_rs,
    rring_ss, rring_rs, rsib_ss, rsib_rs, rx_ss, rx_rs, rdx_ss, rdx_rs, rswap_ss, rswap_rs,
    a2a_ss, a2a_rs, dp_ss, dp_rs, spec_ss, spec_rs,
):
    dp, chan = lax.axis_index("dp"), lax.axis_index("chan")
    core = lax.rem(dp, 2)
    sibling = dp + 1 - 2 * core
    place = ring_place(chan)
    spots = [lax.rem(place + offset, 8) if offset else place for offset in range(8)]
    around = [ring_chan(spot) if offset else chan for offset, spot in enumerate(spots)]
    groups = [lax.rem(spot, 4) for spot in spots]
    group_lanes = [pl.multiple_of(lax.div(spot, 4) * LANES, LANES) for spot in spots]
    nexts = [around[1], around[7]]
    chan_peers = [chan] + [lax.rem(chan + r, N_CHAN) for r in range(1, N_CHAN)]
    dp_peers = [dp] + [lax.rem(dp + r, 4) for r in range(1, 4)]
    across = dp_peers[2]

    def chan_at(offset):
        return around[offset % 8]

    barrier = pltpu.get_barrier_semaphore()
    for r in range(1, N_CHAN):
        pl.semaphore_signal(barrier, inc=1, device_id={"chan": chan_peers[r]}, device_id_type=MESH)
    for r in range(1, 4):
        pl.semaphore_signal(barrier, inc=1, device_id={"dp": dp_peers[r]}, device_id_type=MESH)

    loaded(0, 1, 7, 8, 9, 10, 11, 12, 13, 14, 15, 16)
    pending = []

    def remote(src, dst, send_sem, recv_sem, **device):
        return pltpu.make_async_remote_copy(
            src_ref=src, dst_ref=dst, send_sem=send_sem, recv_sem=recv_sem, device_id=device, device_id_type=MESH
        )

    def send(*args, **device):
        copy = remote(*args, **device)
        copy.start()
        pending.append(copy)

    def exchange(which, source, recv_ref):
        def copy(r):
            peer = chan_peers[r]
            return remote(
                source(peer), recv_ref.at[chan], a2a_ss.at[which, r - 1], a2a_rs.at[which, r - 1], chan=peer
            )

        def start():
            for r in range(1, N_CHAN):
                copy(r).start()

        def wait():
            for r in range(1, N_CHAN):
                copy(r).wait_recv()

        def finish():
            for r in range(1, N_CHAN):
                copy(r).wait_send()

        return start, wait, finish

    def rows_at(number, count):
        return pl.ds(pl.multiple_of(number, ROWS), count)

    def launch(copy):
        copy.start()
        pending.append(copy)

    own_row = dp * ROWS
    pair_row = (dp - core) * ROWS
    away_row = 2 * ROWS - pair_row
    gate_row, gate_away = (core * 2 + lax.div(dp, 2)) * ROWS, (core * 2 + 1 - lax.div(dp, 2)) * ROWS
    gate_pair, gate_other = core * 2 * ROWS, (1 - core) * 2 * ROWS
    half_lanes = pl.multiple_of(core * LANES, LANES)
    other_lanes = pl.multiple_of((1 - core) * LANES, LANES)

    def gate_view(ref):
        return lambda offset, row, count: ref.at[around[offset % 8], rows_at(row, count), :]

    def hidden_view(ref):
        return lambda offset, row, count: ref.at[
            :, groups[offset % 8], rows_at(row, count), pl.ds(group_lanes[offset % 8], LANES)
        ]

    class Ring:
        def __init__(self, which, view, base, count, hook=None):
            self.which, self.view, self.base, self.count, self.hook = which, view, base, count, hook

        def piece(self, turn, step, base):
            half = self.count // 2
            if step == 4:
                return self.view(4, base + turn * half, half)
            return self.view(-TURNS[turn] * step, base, self.count)

        def copy(self, turn, step, ref):
            slot = turn * 4 + step - 1
            return remote(ref, ref, gring_ss.at[self.which, slot], gring_rs.at[self.which, slot], chan=nexts[turn])

        def send(self, turn, step):
            half = self.count // 2
            if step == 4:
                ref = self.view(-TURNS[turn] * 3, self.base + turn * half, half)
            else:
                ref = self.piece(turn, step - 1, self.base)
            launch(self.copy(turn, step, ref))

        def start(self):
            for turn in range(2):
                self.send(turn, 1)

        def step(self, step):
            for turn in range(2):
                self.copy(turn, step, self.piece(turn, step, self.base)).wait_recv()
                if step < 4:
                    self.send(turn, step + 1)
                if self.hook:
                    self.hook(turn, step)

    def slot_of(turn, step):
        return turn * 4 + step - 1 if step else 8

    def gate_sib(base):
        ref = wab_ref.at[:, rows_at(base, 256), :]
        return remote(ref, ref, gsib_ss, gsib_rs, dp=sibling)

    def gate_spread():
        launch(gate_sib(gate_pair))

    def hidden_cross(which, turn, step, base):
        ref, slot = hidden_rings[which].piece(turn, step, base), slot_of(turn, step)
        return remote(ref, ref, gdx_ss.at[which, slot], gdx_rs.at[which, slot], dp=across)

    gate_ring = Ring(0, gate_view(wab_ref), gate_pair, 256)
    def hidden_part(which):
        def view(offset, row, count):
            lanes = pl.ds(group_lanes[offset % 8], LANES)
            return wh_ref.at[which, groups[offset % 8], rows_at(row, count), lanes]

        return Ring(
            1 + which, view, pair_row, 256, lambda turn, step: launch(hidden_cross(which, turn, step, pair_row))
        )

    hidden_rings = up_ring, down_ring = hidden_part(0), hidden_part(1)

    def gate_over(row):
        ref = gate_ring.view(0, row, ROWS)
        return remote(ref, ref, gx_ss, gx_rs, dp=across)

    def swap_copy(row):
        return remote(stage_ref, hidden_view(wh_ref)(0, row, ROWS), gswap_ss, gswap_rs, dp=sibling)

    def gather_prepare():
        gates = jnp.concatenate([wa_ref[...], wb_ref[...]], axis=0).T.astype(BF16)
        wab_ref[chan, rows_at(gate_row, ROWS), :] = gates
        for which, values in enumerate((up_ref[...], down_ref[...].T)):
            first, second = values[:, :LANES], values[:, LANES:]
            kept = jnp.where(core == 0, first, second)
            wh_ref[which, groups[0], rows_at(own_row, ROWS), pl.ds(group_lanes[0], LANES)] = kept.astype(BF16)
            stage_ref[which] = jnp.where(core == 0, second, first).astype(BF16)

    def gather_start():
        launch(swap_copy(own_row))
        launch(gate_over(gate_row))

    def hidden_first():
        swap_copy(sibling * ROWS).wait_recv()
        for which in range(2):
            hidden_rings[which].start()
            launch(hidden_cross(which, 0, 0, pair_row))

    def gate_first():
        gate_over(gate_away).wait_recv()
        gate_ring.start()

    ring_steps = [(0, 0)] + [(turn, step) for step in range(1, 5) for turn in range(2)]

    def gates_arrived():
        gate_sib(gate_other).wait_recv()

    def hidden_arrived(*steps):
        for turn, step in ring_steps:
            if step in steps:
                for which in range(2):
                    hidden_cross(which, turn, step, away_row).wait_recv()

    def beside(ref, j):
        start = 2 * j * ROWS
        return jnp.concatenate(
            [ref[:, start : start + ROWS].astype(F32), ref[:, start + ROWS : start + 2 * ROWS].astype(F32)], axis=0
        ).T

    for j in range(PAIRS):
        packed = beside(tokens_ref, j)
        tok_ref[j * ROWS : (j + 1) * ROWS, :] = packed.astype(BF16)
        for first, values in ((0, packed), (HALF, beside(cotangent_ref, j))):
            low, high = split_pair(values)
            in_send[2 * j, first : first + HALF, :] = low.astype(BF16)
            in_send[2 * j + 1, first : first + HALF, :] = high.astype(BF16)
    in_recv[chan] = in_send[chan]

    lane_id = lax.broadcasted_iota(jnp.int32, (8, LANES), 1)
    row_id = lax.broadcasted_iota(jnp.int32, (8, LANES), 0)
    halves = jnp.where((lane_id >= HALF) == (row_id == 1), 1.0, 0.0) * jnp.where(row_id < 2, 1.0, 0.0)
    halves = halves.astype(BF16)

    def token_sums(parts):
        total = 0.0
        for part in parts:
            total = total + dot_nt(halves, part)
        return [total[h : h + 1, j * ROWS : (j + 1) * ROWS] for h in range(2) for j in range(PAIRS)]

    def split(values):
        high = values.astype(BF16)
        return high, (values - high.astype(F32)).astype(BF16)

    tokens = tok_ref[...]
    wide_tokens = tokens.astype(F32)
    for i, sums in enumerate(token_sums([tokens]) + token_sums(split(wide_tokens * wide_tokens))):
        head_send[i : i + 1, :] = sums

    def row(*refs):
        return jnp.concatenate([ref[...].reshape(1, HALF) for ref in refs], axis=1)

    bup = bup_ref[...].reshape(1, 2 * LANES)
    head_send[16:17, :] = row(ba_ref, bb_ref)
    head_send[17:18, :] = row(gain2_ref, bias2_ref)
    head_send[18:19, :] = row(bdown_ref, bdown_ref)
    head_send[19:20, :] = bup[:, :LANES]
    head_send[20:21, :] = bup[:, LANES:]
    head_send[21:24, :] = jnp.zeros((3, LANES), F32)
    head_recv[chan] = head_send[...]
    head = exchange(0, lambda peer: head_send, head_recv)
    inputs = exchange(1, lambda peer: in_send.at[peer], in_recv)
    gather_prepare()
    pl.semaphore_wait(barrier, N_CHAN - 1 + 3)
    gather_start()
    head[0]()
    hidden_first()

    loaded(4, 5, 17, 21)
    level, filled = bucket_ref[0], items_ref[0]
    coefl_ref[...] = levels_ref[level]
    item_blocks = jnp.where(level == 0, 2, jnp.where(level == 1, 4, 8))
    block_id = 2 * (row_id % PAIRS) + jnp.where(lane_id >= HALF, 1, 0)
    bound = jnp.where(row_id < PAIRS, filled * item_blocks, item_blocks)
    aux_ref[...] = jnp.where(block_id < bound, 1.0, 0.0)
    for i in range(8):
        modes_ref[i] = jnp.concatenate([raw_modes_ref[i], raw_modes_ref[i]], axis=1)
    inputs[0]()
    gate_first()
    log_dt = row(log_dt_ref, log_dt_ref)
    sigma, step_size = 2.0 * jnp.exp(-log_dt), jnp.exp(log_dt)

    base = pl.multiple_of(dp * QUARTER, QUARTER)

    def spec_copy(which, r):
        peer = dp_peers[r]
        src, dst = ((spec_send, spec_recv), (sgrad_send.at[peer], sgrad_recv))[which]
        return remote(src, dst.at[dp], spec_ss.at[which, r - 1], spec_rs.at[which, r - 1], dp=peer)

    cauchy_coefficients(modes_ref, sigma, mcoef_ref)
    cauchy_forward(0, sigma, mcoef_ref, wave_ref, base, sums_ref, spec_send)
    cauchy_forward(1, sigma, mcoef_ref, wave_ref, base, sums_ref, spec_send)
    cauchy_forward(2, sigma, mcoef_ref, wave_ref, base, sums_ref, spec_send)
    cauchy_forward(3, sigma, mcoef_ref, wave_ref, base, sums_ref, spec_send)
    spec_recv[dp] = spec_send[...]
    for r in range(1, 4):
        spec_copy(0, r).start()
    up_ring.step(1)
    gate_ring.step(1)
    down_ring.step(1)

    head[1]()
    sums = head_recv[0, 0:16, :]
    for c in range(1, N_CHAN):
        sums = sums + head_recv[c, 0:16, :]
    mean = sums[0:8] * (1.0 / MODEL_WIDTH)
    rstd = lax.rsqrt(sums[8:16] * (1.0 / MODEL_WIDTH) - mean * mean + EPSILON)

    def columns(rows):
        tall = rows.T
        return [jnp.where(low_lanes(ROWS), tall[:, j : j + 1], tall[:, 4 + j : 5 + j]) for j in range(PAIRS)]

    loaded(2, 3, 6, 18, 19, 20)
    gain1, bias1, skip = row(gain1_ref, gain1_ref), row(bias1_ref, bias1_ref), row(skip_ref, skip_ref)
    mean_cols, rstd_cols = columns(mean), columns(rstd)
    for j in range(PAIRS):
        hat = (tok_ref[j * ROWS : (j + 1) * ROWS, :].astype(F32) - mean_cols[j]) * rstd_cols[j]
        hat_ref[j] = hat
        norm_ref[j] = hat * gain1 + bias1

    spread_pairs(lambda j, rows: norm_ref[j, rows, :], coefl_ref, 0, tw_ref, 0, 5, rhs_ref, False)
    transform_into(sig_ref, mat_ref, 0, rhs_ref, False)

    for r in range(1, 4):
        spec_copy(0, r).wait_recv()
    for source in range(4):
        store_split(rhs_ref, source * QUARTER, 0, spec_recv[source, :QUARTER, :])
        store_split(rhs_ref, ROWS + source * QUARTER, 0, spec_recv[source, QUARTER:, :])
    up_ring.step(2)
    gate_ring.step(2)
    freq_ref[:, 0:256] = split_product(mat_ref, 1, rhs_ref, 0, 256)
    even = split_product(mat_ref, 2, rhs_ref, LANES, LANES)
    freq_ref[:, LANES:256] = jnp.where(low_lanes(256), freq_ref[:, LANES:256], even)
    sign = 1.0 - 2.0 * (lax.broadcasted_iota(jnp.int32, (CHUNK, LANES), 0) % 2).astype(F32)
    nyquist = step_size * column_sum(mcoef_ref[0]) * (1.0 / TOK_DEV)
    down_ring.step(2)

    def store_taps(j, rows, values):
        taps_ref[j, rows, :] = (values + sign * nyquist) * aux_ref[4 + j : 5 + j, :]

    gather_pairs(freq_ref, coefc_ref, 160, tw_ref, 10, 2, store_taps)
    spread_pairs(lambda j, rows: taps_ref[j, rows, :], coefc_ref, 0, tw_ref, 0, 5, rhs_ref, False)
    transform_into(ans_ref, mat_ref, 0, rhs_ref, False)
    multiply_spectra(sig_ref, ans_ref, rhs_ref, False, False)
    transform_into(freq_ref, mat_ref, 1, rhs_ref, False)
    gate_ring.step(3)
    up_ring.step(3)

    def store_conv(j, rows, values):
        conv_ref[j, rows, :] = values
    gather_pairs(freq_ref, coefl_ref, 80, tw_ref, 0, 5, store_conv)
    for j in range(PAIRS):
        mixed = conv_ref[j] * aux_ref[j : j + 1, :] + skip * norm_ref[j]
        cumulative, density = normal_parts(mixed)
        slope_ref[j] = cumulative + mixed * density
        low, high = split_pair(mixed * cumulative)
        acts_send[2 * j] = low.astype(BF16)
        acts_send[2 * j + 1] = high.astype(BF16)
    acts_recv[chan] = acts_send[chan]
    acts = exchange(2, lambda peer: acts_send.at[peer], acts_recv)
    acts[0]()

    def joined(ref, pair, first):
        return join_pair(
            ref[2 * pair, first : first + HALF, :].astype(F32), ref[2 * pair + 1, first : first + HALF, :].astype(F32)
        )

    def lanes_of(pair):
        return slice(pair * LANES, (pair + 1) * LANES)

    def gate_lanes(pair):
        return lanes_of(pair % 2 * 2 + pair // 2)

    def core_copy(which, src, dst):
        return remote(src, dst, core_ss.at[which], core_rs.at[which], dp=sibling)

    def other_core(which, ref):
        return core_copy(which, ref.at[core], ref.at[core])

    def vector(row, first, second):
        return interleave(head_recv[first, 16 + row : 17 + row, :], head_recv[second, 16 + row : 17 + row, :])

    def both_cores(ref):
        return ref[...].reshape(2 * ROWS, MODEL_WIDTH)

    def hidden_group(offset):
        group = groups[offset]
        low, high = 2 * group, 7 - 2 * group
        bias = jnp.concatenate(
            [jnp.where(core == 0, head_recv[c, 19:20, :], head_recv[c, 20:21, :]) for c in (low, high)], axis=1
        )
        pre = dot_nn(both_cores(norm2_ref), wh_ref[0, group]) + bias
        cumulative, density = normal_parts(pre)
        hidden = (pre * cumulative).astype(BF16)
        hid_ref[group] = hidden
        grad = dot_nn(both_cores(gradf_ref), wh_ref[1, group]) * (cumulative + pre * density)
        grad = grad.astype(BF16)
        gpre_ref[group] = grad
        sums = column_sum(grad.astype(F32))
        tail_send[low, pl.ds(3 + core, 1), :] = sums[:, 0:LANES]
        tail_send[high, pl.ds(3 + core, 1), :] = sums[:, LANES : 2 * LANES]
        branch_ref[...] += dot_nt(hidden, wh_ref[1, group]).reshape(2, ROWS, MODEL_WIDTH)
        back2_ref[...] += dot_nt(grad, wh_ref[0, group]).reshape(2, ROWS, MODEL_WIDTH)

    def offset_of(turn, step):
        return TURNS[turn] * (5 - step)

    def far(offset):
        return 4 if offset == -4 else offset

    class RingBack:
        def __init__(self, which, view, base, count, ring_ref, extra):
            self.which, self.view, self.base, self.count = which, view, base, count
            self.ring_ref, self.extra = ring_ref, extra

        def copy(self, turn, step):
            slot = turn * 4 + step - 1
            half = self.count // 2
            if step == 1:
                dst = self.ring_ref.at[slot]
                lead = (slice(None),) * (len(dst.shape) - 2)
                src, dst = self.view(4, self.base + turn * half, half), dst.at[lead + (pl.ds(0, half), slice(None))]
            else:
                src, dst = self.view(offset_of(turn, step), self.base, self.count), self.ring_ref.at[slot]
            return remote(src, dst, rring_ss.at[self.which, slot], rring_rs.at[self.which, slot], chan=nexts[turn])

        def whole(self, offset):
            return self.view(offset, self.base, self.count)[...].astype(F32) + self.extra(offset)

        def step(self, step):
            half = self.count // 2
            if step == 1:
                self.view(4, self.base, self.count)[...] = self.whole(4).astype(BF16)
                for turn in range(2):
                    launch(self.copy(turn, 1))
                return
            for turn in range(2):
                offset, slot = offset_of(turn, step), turn * 4 + step - 2
                total = self.whole(offset)
                self.copy(turn, step - 1).wait_recv()
                if step == 2:
                    parts = [total[..., :half, :], total[..., half:, :]]
                    parts[turn] = parts[turn] + self.ring_ref[slot][..., :half, :].astype(F32)
                    total = jnp.concatenate(parts, axis=-2)
                else:
                    total = total + self.ring_ref[slot].astype(F32)
                self.view(offset, self.base, self.count)[...] = total.astype(BF16)
                launch(self.copy(turn, step))

        def total(self):
            total = self.whole(0)
            for turn in range(2):
                self.copy(turn, 4).wait_recv()
                total = total + self.ring_ref[turn * 4 + 3].astype(F32)
            return total

    waited = set()

    def wait_once(name, copy):
        if name not in waited:
            waited.add(name)
            copy().wait_recv()

    def gate_share():
        ref = gab_w_ref.at[:, rows_at(gate_other, 256), :]
        return remote(ref, sib_ab_ref, rsib_ss, rsib_rs, dp=sibling)

    def gate_extra(offset):
        wait_once("gates", gate_share)
        return sib_ab_ref[around[offset % 8]].astype(F32)

    def cross_copy(pair):
        src = gh_ref.at[:, groups[pair], rows_at(away_row, 256), :]
        return remote(src, cross_ref.at[pair], rdx_ss.at[pair], rdx_rs.at[pair], dp=across)

    def hidden_extra(offset):
        pair = offset % 4
        wait_once(pair, lambda: cross_copy(pair))
        return cross_ref[pair, :, :, pl.ds(group_lanes[offset % 8], LANES)].astype(F32)

    gate_g = RingBack(0, gate_view(gab_w_ref), gate_pair, 256, ring_ab_ref, gate_extra)

    hidden_g = RingBack(1, hidden_view(gh_ref), pair_row, 256, ring_h_ref, hidden_extra)

    def hidden_grads(offset):
        group = groups[offset]
        gh_ref[1, group] = dot_nn(gradf_t_ref[...], hid_ref[group]).astype(BF16)
        gh_ref[0, group] = dot_nn(norm2_t_ref[...], gpre_ref[group]).astype(BF16)
        launch(cross_copy(offset))

    def part_copy():
        return remote(part_ab_ref.at[0], part_ab_ref.at[1], rx_ss, rx_rs, dp=across)

    def last_swap():
        return remote(keep_ref.at[:, rows_at((1 - core) * ROWS, ROWS), :], swap_ref, rswap_ss, rswap_rs, dp=sibling)

    def gate_last():
        gate_total_ref[...] = gate_g.total()
        part_ab_ref[0] = gate_total_ref[rows_at((1 - lax.div(dp, 2)) * ROWS, ROWS), :].astype(BF16)
        launch(part_copy())

    def gate_finish():
        part_copy().wait_recv()
        gw_ref[:, 0:128] = gate_total_ref[rows_at(lax.div(dp, 2) * ROWS, ROWS), :] + part_ab_ref[1].astype(F32)

    def hidden_last():
        keep_ref[...] = hidden_g.total()
        launch(last_swap())
        for which in range(2):
            gw_ref[:, pl.ds(pl.multiple_of(128 + 256 * which + half_lanes, LANES), LANES)] = keep_ref[
                which, rows_at(core * ROWS, ROWS), :
            ]

    def hidden_finish():
        last_swap().wait_recv()
        for which in range(2):
            gw_ref[:, pl.ds(pl.multiple_of(128 + 256 * which + other_lanes, LANES), LANES)] = swap_ref[which]

    late = exchange(4, lambda peer: late_send.at[peer], late_recv)


    def gate_grads(*offsets):
        for offset in offsets:
            c = chan_at(offset)
            gab_w_ref[c] = dot_nn(acts_t_ref[...], gab_ref[c]).astype(BF16)
        if 0 in offsets:
            launch(gate_share())

    def late_messages():
        core_copy(3, half_send.at[1], half_recv.at[1]).wait_recv()
        for p in range(PAIRS):
            out = res_ref[p] + (branch_ref[core, :, lanes_of(p)] + half_recv[1, :, lanes_of(p)].astype(F32)) + interleave(head_recv[2 * p, 18:19, :], head_recv[2 * p + 1, 18:19, :])[0]
            low, high = split_pair(out)
            late_send[2 * p, :HALF, :] = low.astype(BF16)
            late_send[2 * p + 1, :HALF, :] = high.astype(BF16)
        for c in range(N_CHAN):
            late_send[c, ROWS:, :] = jnp.concatenate([tail_send[c], jnp.zeros((8, LANES), F32)], axis=0).astype(BF16)
        late_recv[chan] = late_send[chan]
        late[0]()

    back = exchange(3, lambda peer: back_send.at[peer], back_recv)

    inputs[1]()
    for p in range(PAIRS):
        gradf_ref[core, :, lanes_of(p)] = joined(in_recv, p, HALF).astype(BF16)
    launch(other_core(0, gradf_ref))
    gate_ring.step(4)
    gate_spread()
    down_ring.step(3)
    gates_arrived()
    acts[1]()
    for p in range(PAIRS):
        acts_ref[:, gate_lanes(p)] = joined(acts_recv, p, 0).astype(BF16)

    total = 0.0
    for p in range(PAIRS):
        first = dot_nn(acts_ref[...], wab_ref[2 * p]) + head_recv[2 * p, 16:17, :]
        second = dot_nn(acts_ref[...], wab_ref[2 * p + 1]) + head_recv[2 * p + 1, 16:17, :]
        gate, raw = interleave(first, second)
        swish = lax.logistic(raw)
        gate_ref[p], swish_ref[p] = gate, swish
        resid = joined(in_recv, p, 0) + gate * swish
        res_ref[p] = resid
        total = total + resid
    mean2 = jnp.sum(total, axis=1, keepdims=True) * (1.0 / MODEL_WIDTH)
    total = 0.0
    for p in range(PAIRS):
        centred = res_ref[p] - mean2
        total = total + centred * centred
    rstd2 = lax.rsqrt(jnp.sum(total, axis=1, keepdims=True) * (1.0 / MODEL_WIDTH) + EPSILON)
    gain2 = []
    for p in range(PAIRS):
        gain, bias = vector(1, 2 * p, 2 * p + 1)
        gain2.append(gain)
        hat = (res_ref[p] - mean2) * rstd2
        hat2_ref[p] = hat
        norm2_ref[core, :, lanes_of(p)] = (hat * gain + bias).astype(BF16)
    launch(other_core(1, norm2_ref))
    branch_ref[...] = jnp.zeros_like(branch_ref)
    acts_t_ref[...] = acts_ref[...].astype(F32).T.astype(BF16)
    back2_ref[...] = jnp.zeros_like(back2_ref)
    for c in range(N_CHAN):
        tail_send[c, 3:8, :] = jnp.zeros((5, LANES), F32)
    hidden_arrived(2)
    down_ring.step(4)
    other_core(0, gradf_ref).wait_recv()
    up_ring.step(4)
    gradf_t_ref[...] = both_cores(gradf_ref).astype(F32).T.astype(BF16)
    hidden_arrived(1, 3)
    other_core(1, norm2_ref).wait_recv()
    norm2_t_ref[...] = both_cores(norm2_ref).astype(F32).T.astype(BF16)
    hidden_group(3)
    hidden_group(1)
    hidden_grads(3)
    hidden_arrived(0, 4)
    hidden_group(0)
    hidden_group(2)
    half_send[0] = back2_ref[1 - core].astype(BF16)
    launch(core_copy(2, half_send.at[0], half_recv.at[0]))
    hidden_grads(0)
    half_send[1] = branch_ref[1 - core].astype(BF16)
    launch(core_copy(3, half_send.at[1], half_recv.at[1]))
    core_copy(2, half_send.at[0], half_recv.at[0]).wait_recv()
    back2 = back2_ref[core] + half_recv[0].astype(F32)
    back2_ref[core] = back2

    mean_q, mean_qx = 0.0, 0.0
    for p in range(PAIRS):
        grad, hat = back2_ref[core, :, lanes_of(p)], hat2_ref[p]
        q = grad * gain2[p]
        mean_q = mean_q + q
        mean_qx = mean_qx + q * hat
        gain_grad, bias_grad = interleave(column_sum(grad * hat), column_sum(grad))
        tail_send[2 * p, 1:2, :] = gain_grad
        first, second = interleave(turn_half(column_sum(grad * hat)), turn_half(column_sum(grad)))
        tail_send[2 * p + 1, 1:2, :] = first
    mean_q = jnp.sum(mean_q, axis=1, keepdims=True) * (1.0 / MODEL_WIDTH)
    mean_qx = jnp.sum(mean_qx, axis=1, keepdims=True) * (1.0 / MODEL_WIDTH)
    for p in range(PAIRS):
        hat = hat2_ref[p]
        extra = rstd2 * (back2_ref[core, :, lanes_of(p)] * gain2[p] - mean_q - hat * mean_qx)
        grad_f = joined(in_recv, p, HALF)
        grad_resid = grad_f + extra
        gate, swish = gate_ref[p], swish_ref[p]
        grad_a = (grad_resid * swish).astype(BF16).astype(F32)
        grad_b = (grad_resid * gate * swish * (1.0 - swish)).astype(BF16).astype(F32)
        first, second = interleave(grad_a, grad_b)
        gab_ref[2 * p] = first.astype(BF16)
        gab_ref[2 * p + 1] = second.astype(BF16)
        tail_send[2 * p, 0:1, :] = column_sum(first)
        tail_send[2 * p + 1, 0:1, :] = column_sum(second)
        low, high = interleave(column_sum(grad_f), column_sum(grad_f))
        tail_send[2 * p, 2:3, :] = low
        tail_send[2 * p + 1, 2:3, :] = high
        low, high = split_pair(extra)
        late_send[2 * p, HALF:ROWS, :] = low.astype(BF16)
        late_send[2 * p + 1, HALF:ROWS, :] = high.astype(BF16)
    grad_acts = 0.0
    for c in range(N_CHAN):
        grad_acts = grad_acts + dot_nt(gab_ref[c], wab_ref[c])
    for p in range(PAIRS):
        low, high = split_pair(grad_acts[:, gate_lanes(p)])
        back_send[2 * p] = low.astype(BF16)
        back_send[2 * p + 1] = high.astype(BF16)
    back_recv[chan] = back_send[chan]
    back[0]()
    hidden_grads(1)
    gate_grads(4, 3, -3)
    late_messages()
    gate_grads(2, -2, 1, -1, 0)

    back[1]()
    skip_grad = 0.0
    for j in range(PAIRS):
        grad = joined(back_recv, j, 0) * slope_ref[j]
        slope_ref[j] = grad
        conv_ref[j] = grad * aux_ref[j : j + 1, :]
        skip_grad = skip_grad + column_sum(grad * norm_ref[j])
    hidden_g.step(1)
    gate_g.step(1)
    hidden_grads(2)
    spread_pairs(lambda j, rows: conv_ref[j, rows, :], coefl_ref, 0, tw_ref, 0, 5, rhs_ref, False)
    transform_into(freq_ref, mat_ref, 0, rhs_ref, False)
    multiply_spectra(sig_ref, freq_ref, rhs_ref, True)
    gate_g.step(2)
    hidden_g.step(2)
    transform_into(sig_ref, mat_ref, 1, rhs_ref)

    def store_kernel_grad(j, rows, values):
        taps_ref[j, rows, :] = values * aux_ref[4 + j : 5 + j, :]

    gather_pairs(sig_ref, coefc_ref, 80, tw_ref, 0, 5, store_kernel_grad)
    nyquist_grad = 0.0
    for j in range(PAIRS):
        whole_sign = 1.0 - 2.0 * (lax.broadcasted_iota(jnp.int32, (ROWS, LANES), 0) % 2).astype(F32)
        nyquist_grad = nyquist_grad + column_sum(taps_ref[j] * whole_sign)
    nyquist_grad = fold(nyquist_grad) * (1.0 / TOK_DEV)
    spread_pairs(lambda j, rows: taps_ref[j, rows, :], coefc_ref, 192, tw_ref, 10, 2, rhs_ref)
    taps_freq_ref[...] = split_product(mat_ref, 0, rhs_ref, 0, 256)
    even = split_product(mat_ref, 3, rhs_ref, LANES, LANES)
    taps_freq_ref[:, LANES:256] = jnp.where(low_lanes(256), taps_freq_ref[:, LANES:256], even)
    for source in range(4):
        rows = slice(source * QUARTER, (source + 1) * QUARTER)
        sgrad_send[source, :QUARTER, :] = taps_freq_ref[rows, :]
        sgrad_send[source, QUARTER:, :] = taps_freq_ref[ROWS + source * QUARTER : ROWS + (source + 1) * QUARTER, :]
    sgrad_recv[dp] = sgrad_send[dp]
    for r in range(1, 4):
        spec_copy(1, r).start()
    gate_g.step(3)
    hidden_g.step(3)

    multiply_spectra(ans_ref, freq_ref, rhs_ref, True, False)
    transform_into(freq_ref, mat_ref, 1, rhs_ref, False)
    late[1]()
    gather_pairs(freq_ref, coefl_ref, 80, tw_ref, 0, 5, store_conv)
    gain_grad, bias_grad = 0.0, 0.0
    scaled, crossed = [], []
    for j in range(PAIRS):
        grad = conv_ref[j] + skip * slope_ref[j]
        conv_ref[j] = grad
        gain_grad = gain_grad + column_sum(grad * hat_ref[j])
        bias_grad = bias_grad + column_sum(grad)
    conv = conv_ref[...].reshape(PAIRS * ROWS, LANES) * gain1
    for i, sums in enumerate(
        token_sums(split(conv)) + token_sums(split(conv * hat_ref[...].reshape(PAIRS * ROWS, LANES)))
    ):
        sum_send[i : i + 1, :] = sums
    gate_g.step(4)
    sum_recv[chan] = sum_send[...]
    sums_back = exchange(6, lambda peer: sum_send, sum_recv)

    for r in range(1, 4):
        spec_copy(1, r).wait_recv()
    sgrad_ref[...] = sgrad_recv[0] + sgrad_recv[1] + sgrad_recv[2] + sgrad_recv[3]

    sigma_sum = point_grads(sigma, wave_ref, base, sums_ref, sgrad_ref, pgrad_ref)
    square_sum = mode_sums(0, jnp.zeros_like(sigma_sum), sigma, mcoef_ref, wave_ref, base, pgrad_ref, mback_ref)
    sums_back[0]()
    hidden_g.step(4)
    square_sum = mode_sums(1, square_sum, sigma, mcoef_ref, wave_ref, base, pgrad_ref, mback_ref)
    gate_last()
    square_sum = mode_sums(2, square_sum, sigma, mcoef_ref, wave_ref, base, pgrad_ref, mback_ref)
    square_sum = mode_sums(3, square_sum, sigma, mcoef_ref, wave_ref, base, pgrad_ref, mback_ref)
    mode_grads, dt_grad = mode_gradients(modes_ref, sigma, nyquist_grad, step_size, sigma_sum, square_sum, mback_ref)
    mask = low_lanes(32)
    for i in range(4):
        dp_send[i * 32 : (i + 1) * 32, :] = jnp.where(mask, mode_grads[i], mode_grads[i + 4])
    first = low_lanes(1)
    dp_send[128:129, :] = jnp.where(first, dt_grad, fold(skip_grad))
    dp_send[129:130, :] = jnp.where(first, fold(gain_grad), fold(bias_grad))
    dp_send[130:136, :] = jnp.zeros((6, LANES), F32)
    tail_sum = late_recv[0, ROWS:, :].astype(F32)
    for c in range(1, N_CHAN):
        tail_sum = tail_sum + late_recv[c, ROWS:, :].astype(F32)
    dp_send[136:144, :] = tail_sum[:8]
    dp_low[...] = dp_send[...].astype(BF16)

    def dp_copy(r):
        return remote(dp_low, dp_recv.at[r - 1], dp_ss.at[r - 1], dp_rs.at[r - 1], dp=dp_peers[r])

    for r in range(1, 4):
        dp_copy(r).start()
    gate_finish()

    sums_back[1]()
    sums = sum_recv[0]
    for c in range(1, N_CHAN):
        sums = sums + sum_recv[c]
    hidden_last()
    sums = sums * (1.0 / MODEL_WIDTH)
    rstd_cols, q_cols, qx_cols = columns(rstd), columns(sums[0:8]), columns(sums[8:16])
    for j in range(PAIRS):
        rows = slice(j * ROWS, (j + 1) * ROWS)
        out_ref[rows, :] = joined(late_recv, j, 0).astype(BF16)
        dtok_ref[rows, :] = joined(late_recv, j, HALF) + rstd_cols[j] * (
            conv_ref[j] * gain1 - q_cols[j] - hat_ref[j] * qx_cols[j]
        )
    for r in range(1, 4):
        dp_copy(r).wait_recv()
    total = dp_send[...] + (dp_recv[0].astype(F32) + dp_recv[1].astype(F32) + dp_recv[2].astype(F32))
    hidden_finish()
    gm_ref[...] = total[0:128]
    gv_ref[...] = total[128:144]
    for copy in pending:
        copy.wait_send()
    for group in (head, inputs, acts, back, late, sums_back):
        group[2]()
    for r in range(1, 4):
        dp_copy(r).wait_send()
        spec_copy(0, r).wait_send()
        spec_copy(1, r).wait_send()
def block_entry(bucket_ref, items_ref, *refs):
    n_in, n_out = 22, 5
    given, results = refs[:n_in], refs[n_in : n_in + n_out]
    held = refs[n_in + n_out : 2 * n_in + n_out]
    made = refs[2 * n_in + n_out : 2 * (n_in + n_out)]
    scratch, in_sem, out_sem = refs[2 * (n_in + n_out) : -2], refs[-2], refs[-1]

    def load(number):
        return pltpu.make_async_copy(given[number], held[number], in_sem.at[number])

    def loaded(*numbers):
        for number in numbers:
            load(number).wait()

    for number in (0, 7, 9, 13, 15, 1, 8, 10, 11, 12, 14, 16, 4, 5, 21, 17, 2, 3, 6, 18, 20, 19):
        load(number).start()
    block_kernel(loaded, bucket_ref, items_ref, *held, *made, *scratch)
    copies = [pltpu.make_async_copy(made[n], results[n], out_sem.at[n]) for n in range(n_out)]
    for copy in copies:
        copy.start()
    for copy in copies:
        copy.wait()


def unpack_entry(*refs):
    n_in, n_out = 6, 17
    given, results = refs[:n_in], refs[n_in : n_in + n_out]
    held = refs[n_in + n_out : 2 * n_in + n_out]
    made, in_sem, out_sem = refs[2 * n_in + n_out : -2], refs[-2], refs[-1]
    loads = [pltpu.make_async_copy(given[n], held[n], in_sem.at[n]) for n in range(n_in)]
    stores = [pltpu.make_async_copy(made[n], results[n], out_sem.at[n]) for n in range(n_out)]
    for copy in loads:
        copy.start()
    for copy in loads:
        copy.wait()
    unpack_kernel(*held, *made)
    for copy in stores:
        copy.start()
    for copy in stores:
        copy.wait()


def unpack_kernel(
    out_ref, dtok_ref, gw_ref, gm_ref, gv_ref, cotangent_ref,
    output_ref, tokens_ref, gain1_ref, bias1_ref, modes_ref, dt_ref, skip_ref, wa_ref, ba_ref, wb_ref, bb_ref,
    gain2_ref, bias2_ref, up_ref, bup_ref, down_ref, bdown_ref,
):
    for j in range(PAIRS):
        out = out_ref[j * ROWS : (j + 1) * ROWS, :].astype(F32).T.astype(BF16)
        grad = dtok_ref[j * ROWS : (j + 1) * ROWS, :].T
        for h in range(2):
            lanes, rows = slice((2 * j + h) * ROWS, (2 * j + h + 1) * ROWS), slice(h * HALF, (h + 1) * HALF)
            output_ref[:, lanes] = out[rows]
            tokens_ref[:, lanes] = cotangent_ref[:, lanes] + grad[rows]
    for i in range(8):
        modes_ref[i] = gm_ref[i % 4 * 32 : i % 4 * 32 + 32, i // 4 * HALF : (i // 4 + 1) * HALF]
    gates = gw_ref[:, :LANES].T
    wa_ref[...] = gates[:HALF]
    wb_ref[...] = gates[HALF:]
    up_ref[...] = gw_ref[:, 128:384]
    down_ref[...] = gw_ref[:, 384:640].T
    for at, low, high in (
        (0, dt_ref, skip_ref), (1, gain1_ref, bias1_ref), (8, ba_ref, bb_ref), (9, gain2_ref, bias2_ref),
    ):
        low[...] = gv_ref[at, :HALF]
        high[...] = gv_ref[at, HALF:]
    bdown_ref[...] = gv_ref[10, :HALF]
    bup_ref[:LANES] = gv_ref[11, :]
    bup_ref[LANES:] = gv_ref[12, :]


def block_program():
    mats, twiddle, levels, constant, wave = mixer_tables()

    def run(tokens, cotangent, bucket, items, gain1, bias1, modes, log_dt, skip, w_a, b_a, w_b, b_b, gain2, bias2, w_up, b_up, w_down, b_down):
        anywhere = pl.BlockSpec(memory_space=pl.ANY)
        smem = pl.BlockSpec(memory_space=pltpu.SMEM)
        dma = pltpu.SemaphoreType.DMA

        def buf(*shape):
            return pltpu.VMEM(shape, F32)

        def low(*shape):
            return pltpu.VMEM(shape, BF16)

        def full(*shape):
            return jax.ShapeDtypeStruct(shape, F32)

        big, wide = (PAIRS, ROWS, LANES), (256, WIDE)
        def like(arrays):
            return [pltpu.VMEM(tuple(a.shape), a.dtype) for a in arrays]

        arguments = (
            tokens.T, cotangent.T, gain1, bias1, jnp.swapaxes(modes, 1, 2), log_dt, skip, w_a.T, b_a, w_b.T, b_b, gain2,
            bias2, w_up, b_up, w_down, b_down, levels, constant, mats, twiddle, wave,
        )
        middle = (
            jax.ShapeDtypeStruct((512, LANES), BF16), full(512, LANES), full(ROWS, WIDE), full(ROWS, LANES),
            full(16, LANES),
        )
        packed = pl.pallas_call(
            block_entry,
            out_shape=middle,
            in_specs=[smem] * 2 + [anywhere] * 22,
            out_specs=(anywhere,) * 5,
            scratch_shapes=like(arguments) + like(middle) + [
                low(512, LANES), buf(8, LANES), buf(160, LANES), buf(8, 32, LANES),
                low(N_CHAN, 512, 128), low(2, 4, 512, 256), low(N_CHAN, 512, 128), low(2, 4, 512, 256),
                low(2, ROWS, LANES), low(N_CHAN, 256, LANES), low(8, 256, LANES), low(8, 2, 256, LANES), low(2, ROWS, LANES),
                low(4, 2, 256, 256), buf(2, 256, LANES), buf(2, ROWS, LANES), buf(256, LANES),
                low(N_CHAN, ROWS, LANES), low(N_CHAN, ROWS, LANES), buf(24, LANES), buf(N_CHAN, 24, LANES),
                low(N_CHAN, HALF, LANES), low(N_CHAN, HALF, LANES), low(N_CHAN, HALF, LANES), low(N_CHAN, HALF, LANES),
                low(N_CHAN, 144, LANES), low(N_CHAN, 144, LANES),
                buf(16, LANES), buf(N_CHAN, 16, LANES), buf(N_CHAN, 8, LANES),
                buf(144, LANES), low(144, LANES), low(3, 144, LANES), buf(64, 256), buf(4, 64, 256), buf(4, 64, 256), buf(4, 64, 256),
                buf(*big), buf(*big), buf(*big), buf(*big), low(2, *wide), buf(*wide), buf(*wide), buf(*wide), buf(*big),
                buf(10, 32, LANES), buf(2, 16, QUARTER, LANES), buf(2, 16, QUARTER, LANES), buf(10, 32, LANES),
                buf(64, 256), buf(256, 256),
                buf(*big), buf(*big), buf(*big), buf(*big), low(ROWS, 512), low(2, ROWS, 512), low(2, ROWS, 512),
                buf(2, ROWS, 512), buf(2, ROWS, 512), low(2, ROWS, 512), low(2, ROWS, 512),
                low(N_CHAN, ROWS, LANES), low(4, 256, 256), low(4, 256, 256), low(512, ROWS), low(512, 256), low(512, 256),
                dma((3, 8)), dma((3, 8)), dma, dma, dma, dma, dma((2, 9)), dma((2, 9)), dma, dma, dma((4,)), dma((4,)),
                dma((2, 8)), dma((2, 8)), dma, dma, dma, dma, dma((4,)), dma((4,)), dma, dma,
                dma((7, 7)), dma((7, 7)), dma((3,)), dma((3,)), dma((2, 3)), dma((2, 3)), dma((22,)), dma((5,)),
            ],
            compiler_params=pltpu.CompilerParams(
                collective_id=0, has_side_effects=True, vmem_limit_bytes=60 * 1024 * 1024
            ),
            name="block",
        )(bucket, items, *arguments)
        small = full(HALF)
        final = (
                jax.ShapeDtypeStruct((HALF, TOK_DEV), BF16), full(HALF, TOK_DEV), small, small, full(8, 32, HALF),
                small, small, full(HALF, ROWS), small, full(HALF, ROWS), small, small, small, full(ROWS, 256),
                full(256), full(256, ROWS), small,
            )
        sources = (*packed, cotangent.T)
        results = pl.pallas_call(
            unpack_entry,
            out_shape=final,
            in_specs=[anywhere] * 6,
            out_specs=(anywhere,) * 17,
            scratch_shapes=like(sources) + like(final) + [dma((6,)), dma((17,))],
            name="unpack",
        )(*sources)
        turned = {0, 1, 4, 7, 9}
        return tuple(jnp.swapaxes(r, -1, -2) if i in turned else r for i, r in enumerate(results))

    return run


def solution(mesh):
    small = mesh.shape["chan"] == N_CHAN and mesh.shape["dp"] == 4
    return jax.shard_map(
        block_program() if small else shards,
        mesh=mesh,
        in_specs=(
            P("dp", "chan"),
            P("dp", "chan"),
            P("dp"),
            P("dp"),
            P("chan"),
            P("chan"),
            P(None, "chan", None),
            P("chan"),
            P("chan"),
            P("dp", "chan"),
            P("chan"),
            P("dp", "chan"),
            P("chan"),
            P("chan"),
            P("chan"),
            P("dp", "chan"),
            P("chan"),
            P("chan", "dp"),
            P("chan"),
        ),
        out_specs=(
            P("dp", "chan"),
            P("dp", "chan"),
            P("chan"),
            P("chan"),
            P(None, "chan", None),
            P("chan"),
            P("chan"),
            P("dp", "chan"),
            P("chan"),
            P("dp", "chan"),
            P("chan"),
            P("chan"),
            P("chan"),
            P("dp", "chan"),
            P("chan"),
            P("chan", "dp"),
            P("chan"),
        ),
        check_vma=False,
    )
```

profile of v0, /device:TPU:0, one launch (start us, length us, event | category | flops | bytes accessed | tf_op | source)
XLA Modules:
  0.0 81.3 jit_solution(16440666107444571012)
XLA Ops:
  2.0 76.8 %block.1 = (bf16[512,128]{1,0:T(8,128)(2,1)}, f32[512,128]{1,0:T(8,128)}, f32[128,640]{1,0:T(8,128)}, f32[128,128]{1,0:T(8,128)}, f32[16,128]{1,0:T(8,128)}) custom-call(s32[1]{0:T(128)S(6)} %copy.41.bucket_ref, s32[1]{0:T(128)S(6)} %copy.42.items_ref, bf16[64,1024]{1,0:T(8,128)(2,1)} %bitcast.12, f32[64,1024]{1,0:T(8,128)} %bitcast.10, f32[64]{0:T(128)} %refs_2_.1, ...), custom_call_target="tpu_custom_call" | custom-call | tf_op jit(solution)/shard_map/block/pallas_call | solution.py:1674
  78.8 2.6 %unpack.1 = (bf16[64,1024]{1,0:T(8,128)(2,1)}, f32[64,1024]{1,0:T(8,128)}, f32[64]{0:T(128)}, f32[64]{0:T(128)}, f32[8,32,64]{2,1,0:T(8,128)}, /*index=5*/f32[64...) custom-call(bf16[512,128]{1,0:T(8,128)(2,1)} %get-tuple-element.39.r, ...), custom_call_target="tpu_custom_call" | custom-call | tf_op jit(solution)/shard_map/unpack/pallas_call | solution.py:1711
where the time goes:
time: 81.5 us; the launch traced here: 81.3 us
  Pallas kernels  79.4 us (97%)
  between operations  1.96 us (2%)
    pallas_call x1, Pallas kernels, run(): pl.pallas_call(block_entry, out_shape=middle, in_specs=[smem] * 2 + [anyw...  76.8 us
    pallas_call x1, Pallas kernels, run(): pl.pallas_call(unpack_entry, out_shape=final, in_specs=[anywhere] * 6, ou...  2.55 us

commit v1 on v0

--- a/solution.py
+++ b/solution.py
@@ -817,7 +817,7 @@
 
 
 def block_kernel(
-    loaded, bucket_ref, items_ref, tokens_ref, cotangent_ref, gain1_ref, bias1_ref, raw_modes_ref, log_dt_ref, skip_ref,
+    bring_in, loaded, bucket_ref, items_ref, tokens_ref, cotangent_ref, gain1_ref, bias1_ref, raw_modes_ref, log_dt_ref, skip_ref,
     wa_ref, ba_ref, wb_ref, bb_ref, gain2_ref, bias2_ref, up_ref, bup_ref, down_ref, bdown_ref,
     levels_ref, coefc_ref, mat_ref, tw_ref, wave_ref,
     out_ref, dtok_ref, gw_ref, gm_ref, gv_ref,
@@ -856,6 +856,7 @@
     for r in range(1, 4):
         pl.semaphore_signal(barrier, inc=1, device_id={"dp": dp_peers[r]}, device_id_type=MESH)
 
+    bring_in()
     loaded(0, 1, 7, 8, 9, 10, 11, 12, 13, 14, 15, 16)
     pending = []
 
@@ -1585,9 +1586,11 @@
         for number in numbers:
             load(number).wait()
 
-    for number in (0, 7, 9, 13, 15, 1, 8, 10, 11, 12, 14, 16, 4, 5, 21, 17, 2, 3, 6, 18, 20, 19):
-        load(number).start()
-    block_kernel(loaded, bucket_ref, items_ref, *held, *made, *scratch)
+    def bring_in():
+        for number in (0, 7, 9, 13, 15, 1, 8, 10, 11, 12, 14, 16, 4, 5, 21, 17, 2, 3, 6, 18, 20, 19):
+            load(number).start()
+
+    block_kernel(bring_in, loaded, bucket_ref, items_ref, *held, *made, *scratch)
     copies = [pltpu.make_async_copy(made[n], results[n], out_sem.at[n]) for n in range(n_out)]
     for copy in copies:
         copy.start()

time: 81.5 us -> 81.5 us (level)
  no operation moved by 1% of the time
where the time goes in v1:
time: 81.5 us; the launch traced here: 81.3 us
  Pallas kernels  79.4 us (97%)
  between operations  1.96 us (2%)
    pallas_call x1, Pallas kernels, run(): pl.pallas_call(block_entry, out_shape=middle, in_specs=[smem] * 2 + [anyw...  76.8 us
    pallas_call x1, Pallas kernels, run(): pl.pallas_call(unpack_entry, out_shape=final, in_specs=[anywhere] * 6, ou...  2.55 us

profile of v1, /device:TPU:0, one launch (start us, length us, event | category | flops | bytes accessed | tf_op | source)
XLA Modules:
  0.0 81.3 jit_solution(14666162549918674644)
XLA Ops:
  2.0 76.8 %block.1 = (bf16[512,128]{1,0:T(8,128)(2,1)}, f32[512,128]{1,0:T(8,128)}, f32[128,640]{1,0:T(8,128)}, f32[128,128]{1,0:T(8,128)}, f32[16,128]{1,0:T(8,128)}) custom-call(s32[1]{0:T(128)S(6)} %copy.41.bucket_ref, s32[1]{0:T(128)S(6)} %copy.42.items_ref, bf16[64,1024]{1,0:T(8,128)(2,1)} %bitcast.12, f32[64,1024]{1,0:T(8,128)} %bitcast.10, f32[64]{0:T(128)} %refs_2_.1, ...), custom_call_target="tpu_custom_call" | custom-call | tf_op jit(solution)/shard_map/block/pallas_call | solution.py:1677
  78.8 2.6 %unpack.1 = (bf16[64,1024]{1,0:T(8,128)(2,1)}, f32[64,1024]{1,0:T(8,128)}, f32[64]{0:T(128)}, f32[64]{0:T(128)}, f32[8,32,64]{2,1,0:T(8,128)}, /*index=5*/f32[64...) custom-call(bf16[512,128]{1,0:T(8,128)(2,1)} %get-tuple-element.39.r, ...), custom_call_target="tpu_custom_call" | custom-call | tf_op jit(solution)/shard_map/unpack/pallas_call | solution.py:1714
